TPU v7x, 32 devices: a whole 2x2x4 slice. The times are simulated.
32 devices in a mesh: ctx: 8 (over z, x), tp: 4 (over y, core).
Axes of the slice: x: 2, y: 2, z: 4, core: 2. Of those that a mesh axis runs over, the one named last changes fastest.
Arguments:
- queries: bfloat16 [1024, 2048], P('ctx', 'tp'), may hold values from -6 to 6
- key_rows: bfloat16 [1024, 512], P('ctx', 'tp'), may hold values from -6 to 6
- value_matrix: bfloat16 [1024, 512], P('ctx', 'tp'), may hold values from -6 to 6
- attention_out: bfloat16 [1024, 2048], P('ctx', 'tp'), may hold values from -6 to 6
- output_grad: bfloat16 [1024, 2048], P('ctx', 'tp'), may hold values from -6 to 6
- w_query: bfloat16 [2048, 2048], P(None, 'tp'), may hold values from -3 to 3
- key_weight: bfloat16 [2048, 512], P(None, 'tp'), may hold values from -3 to 3
- value_weight: bfloat16 [2048, 512], P(None, 'tp'), may hold values from -3 to 3
- span_pos: int32 [16], replicated, may hold values from 0 to 15, as said below
Outputs:
- input_grad: bfloat16 [1024, 2048], P('ctx', 'tp')
Inputs may be any that keep to these rules, and one draw needn't show every extreme that they name: Device d of ctx stores spans 2d and 2d + 1; their positions span_pos[2d] and span_pos[2d + 1] add up to 15, in either order; every position appears once.
All inputs are finite; a program needn't handle non-finite values.
Results may differ from a plain program's by a relative error of at most 0.0056.
Values may be sent and summed in bfloat16 or wider, within the bound.
A program may use at most 64 MiB of HBM per device.

v0:
```python
import jax
import jax.numpy as jnp
from jax import lax
from jax.sharding import PartitionSpec as P

HEAD_SIZE = 128


def contract_last(left, right):
    return lax.dot_general(
        left, right, (((1,), (1,)), ((), ())), preferred_element_type=jnp.float32
    )


def contract_first(left, right):
    return lax.dot_general(
        left, right, (((0,), (0,)), ((), ())), preferred_element_type=jnp.float32
    )


def block_stats(query, query_pos, key_part, key_pos, running):
    run_max, run_sum = running
    raw_scores = contract_last(query, key_part) * HEAD_SIZE ** (-0.5)
    allowed = key_pos[None, :] <= query_pos[:, None]
    masked = jnp.where(allowed, raw_scores, -jnp.inf)
    new_max = jnp.maximum(run_max, jnp.max(masked, axis=1))
    run_sum = run_sum * jnp.exp(run_max - new_max) + jnp.sum(
        jnp.exp(masked - new_max[:, None]), axis=1
    )
    return (new_max, run_sum)


def block_grads(query, query_pos, grad_rows, log_totals, deltas, key_part, value_part, key_pos):
    score_scale = HEAD_SIZE ** (-0.5)
    raw_scores = contract_last(query, key_part) * score_scale
    allowed = key_pos[None, :] <= query_pos[:, None]
    weights = jnp.where(allowed, jnp.exp(raw_scores - log_totals[:, None]), 0.0)
    probs_low = weights.astype(jnp.bfloat16)
    grad_probs = contract_last(grad_rows, value_part)
    grad_scores = (weights * (grad_probs - deltas[:, None])).astype(jnp.bfloat16)
    part_query = jnp.dot(grad_scores, key_part, preferred_element_type=jnp.float32) * score_scale
    part_key = contract_first(grad_scores, query) * score_scale
    part_value = contract_first(probs_low, grad_rows)
    return (part_query, part_key, part_value)


def local(
    queries,
    key_rows,
    value_matrix,
    attention_out,
    output_grad,
    w_query,
    key_weight,
    value_weight,
    span_pos,
):
    tok_rows = queries.shape[0]
    span_len = tok_rows // 2
    group_width = queries.shape[1] // HEAD_SIZE
    query_count = span_len * group_width
    cycle_size = lax.axis_size("ctx")
    my_index = lax.axis_index("ctx")
    offsets = jnp.arange(span_len, dtype=jnp.int32)
    own_pos = lax.dynamic_slice_in_dim(span_pos, 2 * my_index, 2)
    query_parts, grad_parts, deltas, query_pos = ([], [], [], [])
    for half_index in range(2):
        low = half_index * span_len
        grad_half = output_grad[low : low + span_len].reshape(query_count, HEAD_SIZE)
        out_half = attention_out[low : low + span_len].reshape(query_count, HEAD_SIZE)
        query_parts.append(queries[low : low + span_len].reshape(query_count, HEAD_SIZE))
        grad_parts.append(grad_half)
        deltas.append(jnp.sum(grad_half.astype(jnp.float32) * out_half.astype(jnp.float32), axis=1))
        query_pos.append(jnp.repeat(own_pos[half_index] * span_len + offsets, group_width))
    start_stats = (
        jnp.full((query_count,), -jnp.inf, jnp.float32),
        jnp.zeros((query_count,), jnp.float32),
    )
    zero_rows = jnp.zeros((query_count, HEAD_SIZE), jnp.float32)
    keys_all, values_all = (
        lax.all_gather(key_rows, "ctx", axis=0, tiled=True),
        lax.all_gather(value_matrix, "ctx", axis=0, tiled=True),
    )
    total_rows = keys_all.shape[0]
    span_total = 2 * cycle_size
    span_ids = jnp.arange(span_total, dtype=jnp.int32)
    inverse = jnp.sum(
        jnp.where(span_pos[None, :] == span_ids[:, None], span_ids[None, :], 0), axis=1
    )
    sorted_keys = keys_all.reshape(span_total, span_len, HEAD_SIZE)[inverse].reshape(
        total_rows, HEAD_SIZE
    )
    sorted_values = values_all.reshape(span_total, span_len, HEAD_SIZE)[inverse].reshape(
        total_rows, HEAD_SIZE
    )
    key_block = min(1024, total_rows)
    block_offsets = jnp.arange(key_block, dtype=jnp.int32)
    log_totals = []
    block_counts = []
    for half_index in range(2):
        block_count = (own_pos[half_index] * span_len + span_len - 1) // key_block + 1
        block_counts.append(block_count)

        def sorted_stats(block_index, running):
            first_row = block_index * key_block
            key_part = lax.dynamic_slice_in_dim(sorted_keys, first_row, key_block, 0)
            return block_stats(
                query_parts[half_index],
                query_pos[half_index],
                key_part,
                first_row + block_offsets,
                running,
            )

        run_max, run_sum = lax.fori_loop(0, block_count, sorted_stats, start_stats)
        log_totals.append(run_max + jnp.log(run_sum))
    key_acc = jnp.zeros((total_rows, HEAD_SIZE), jnp.float32)
    value_acc = jnp.zeros((total_rows, HEAD_SIZE), jnp.float32)
    query_accs = []
    for half_index in range(2):

        def sorted_grads(block_index, loop_state):
            query_acc, key_acc, value_acc = loop_state
            first_row = block_index * key_block
            key_part = lax.dynamic_slice_in_dim(sorted_keys, first_row, key_block, 0)
            value_part = lax.dynamic_slice_in_dim(sorted_values, first_row, key_block, 0)
            part_query, part_key, part_value = block_grads(
                query_parts[half_index],
                query_pos[half_index],
                grad_parts[half_index],
                log_totals[half_index],
                deltas[half_index],
                key_part,
                value_part,
                first_row + block_offsets,
            )
            key_acc = lax.dynamic_update_slice_in_dim(
                key_acc,
                lax.dynamic_slice_in_dim(key_acc, first_row, key_block, 0) + part_key,
                first_row,
                0,
            )
            value_acc = lax.dynamic_update_slice_in_dim(
                value_acc,
                lax.dynamic_slice_in_dim(value_acc, first_row, key_block, 0) + part_value,
                first_row,
                0,
            )
            return (query_acc + part_query, key_acc, value_acc)

        query_acc, key_acc, value_acc = lax.fori_loop(
            0, block_counts[half_index], sorted_grads, (zero_rows, key_acc, value_acc)
        )
        query_accs.append(query_acc)
    key_stored = key_acc.reshape(span_total, span_len, HEAD_SIZE)[span_pos].reshape(
        total_rows, HEAD_SIZE
    )
    value_stored = value_acc.reshape(span_total, span_len, HEAD_SIZE)[span_pos].reshape(
        total_rows, HEAD_SIZE
    )
    key_grad, value_grad = (
        lax.psum_scatter(key_stored, "ctx", scatter_dimension=0, tiled=True),
        lax.psum_scatter(value_stored, "ctx", scatter_dimension=0, tiled=True),
    )
    grad_query = jnp.concatenate(
        [acc_part.reshape(span_len, group_width * HEAD_SIZE) for acc_part in query_accs], axis=0
    ).astype(jnp.bfloat16)
    grad_key = key_grad.astype(jnp.bfloat16)
    grad_value = value_grad.astype(jnp.bfloat16)
    partial_sum = (
        contract_last(grad_query, w_query)
        + contract_last(grad_key, key_weight)
        + contract_last(grad_value, value_weight)
    )
    return lax.psum_scatter(partial_sum, "tp", scatter_dimension=1, tiled=True).astype(jnp.bfloat16)


def solution(mesh):
    in_specs = (
        P("ctx", "tp"),
        P("ctx", "tp"),
        P("ctx", "tp"),
        P("ctx", "tp"),
        P("ctx", "tp"),
        P(None, "tp"),
        P(None, "tp"),
        P(None, "tp"),
        P(),
    )
    out_specs = P("ctx", "tp")
    return jax.shard_map(local, mesh=mesh, in_specs=in_specs, out_specs=out_specs, check_vma=False)
```

profile of v0, /device:TPU:0, one launch (start us, length us, event | category | flops | bytes accessed | tf_op | source)
XLA Modules:
  0.0 261.6 jit_solution(2533232982897634380)
XLA Ops:
  6.5 0.9 dynamic_slice.3
  8.7 0.8 select_reduce_fusion
  10.2 1.2 compare_select_fusion
  11.4 32.7 %all_gather.6 = bf16[1024,128]{1,0:T(8,128)(2,1)S(1)} all-gather(bf16[128,128]{1,0:T(8,128)(2,1)} %param.18), channel_id=1, replica_groups=mesh['ctx'=8,'tp'=4] {'ctx'}, dimensions={0}, use_global_device_ids=true | all-gather | bytes 294912 | tf_op jit(solution)/shard_map/all_gather | solution.py:81
  44.1 1.5 fusion.45
  46.3 1.0 while.56
  47.3 0.7 fusion.44
  48.1 0.7 slice_convert_fusion
  48.8 30.7 %all_gather.7 = bf16[1024,128]{1,0:T(8,128)(2,1)S(1)} all-gather(bf16[128,128]{1,0:T(8,128)(2,1)S(1)} %copy-done.16), channel_id=1, replica_groups=mesh['ctx'=8,'tp'=4] {'ctx'}, dimensions={0}, use_global_device_ids=true | all-gather | bytes 294912 | tf_op jit(solution)/shard_map/all_gather | solution.py:82
  80.9 0.7 broadcast_in_dim.59.clone
  81.6 3.9 %while.57 = (s32[]{:T(128)}, f32[256,128]{1,0:T(8,128)}, f32[1024,128]{1,0:T(8,128)S(1)}, f32[1024,128]{1,0:T(8,128)S(1)}, s32[]{:T(128)}, /*index=5*/bf16[256,1...) while((s32[]{:T(128)}, f32[256,128]{1,0:T(8,128)}, ...), condition=%wide.region_7.8_spmd.clone, body=%wide.region_6.7_spmd.clone.sunk | while | flops 338101248 | bytes 10500613 | solution.py:151
  81.8 1.4 fusion.119
  85.5 0.9 reshape.97
  86.4 1.9 while.58
  86.6 1.3 fusion.125
  88.9 0.9 reshape.98
  89.8 1.6 reshape.105
  91.4 1.0 multiply_reduce_fusion
  92.4 0.7 broadcast_in_dim.59
  93.1 3.9 %while.59 = (s32[]{:T(128)}, f32[256,128]{1,0:T(8,128)}, f32[1024,128]{1,0:T(8,128)S(1)}, f32[1024,128]{1,0:T(8,128)S(1)}, s32[]{:T(128)}, /*index=5*/bf16[256,1...) while((s32[]{:T(128)}, f32[256,128]{1,0:T(8,128)}, ...), condition=%wide.region_14.15_spmd.clone, body=%wide.region_13.14_spmd.clone.sunk | while | flops 338101248 | bytes 10500613 | solution.py:151
  93.3 1.4 fusion.136
  96.0 0.6 copy-done.5
  97.0 0.6 pad_clamp_fusion
  97.7 1.4 gather_fusion.2
  99.1 1.4 gather_fusion.3
  100.8 0.8 fusion.34
  101.6 60.5 %reduce-scatter.4.cloned.1.call-done = f32[128,128]{1,0:T(8,128)} async-done(((f32[1024,128]{1,0:T(8,128)}), f32[128,128]{1,0:T(8,128)}) %reduce-scatter.4.cloned.1.call-update) | async-done | bytes 65552 | tf_op jit(solution)/shard_map/reduce_scatter | solution.py:162
  162.0 2.3 convolution_add_fusion.3
  164.4 62.4 %reduce-scatter.6.cloned.1.call-done = f32[128,128]{1,0:T(8,128)} async-done(((f32[1024,128]{1,0:T(8,128)}), f32[128,128]{1,0:T(8,128)}) %reduce-scatter.6.cloned.1.call-update) | async-done | bytes 65552 | tf_op jit(solution)/shard_map/reduce_scatter | solution.py:163
  226.7 2.7 %convolution_add_fusion.2 = f32[128,2048]{1,0:T(8,128)} fusion(f32[128,2048]{1,0:T(8,128)} %convolution_add_fusion.3, bf16[2048,128]{1,0:T(8,128)(2,1)} %param.24, f32[128,128]{1,0:T(8,128)} %reduce-scatter.6.cloned.1.call-done), kind=kOutput, calls=%fused_computation.50 | convolution fusion | flops 67387392 | bytes 2686976 | tf_op jit(solution)/shard_map/dot_general | solution.py:10
  229.4 24.0 %reduce-scatter.8.cloned.1.call-done = f32[128,512]{1,0:T(8,128)} async-done(((f32[128,2048]{1,0:T(8,128)}), f32[128,512]{1,0:T(8,128)}) %reduce-scatter.8.cloned.1.call-update) | async-done | bytes 262160 | tf_op jit(solution)/shard_map/reduce_scatter | solution.py:175
  253.5 1.6 convert_element_type.48
  (91 shorter events, 9.2 us)
Async XLA Ops:
  6.5 94.2 %copy-start = (bf16[2048,512]{1,0:T(8,128)(2,1)S(1)}, bf16[2048,512]{1,0:T(8,128)(2,1)}, u32[]{:S(2)}) copy-start(bf16[2048,512]{1,0:T(8,128)(2,1)} %param.22) | copy-start | bytes 6291460
  6.5 155.5 %reduce-scatter.4.cloned.1.call-start = ((), (), s32[]{:S(2)}) async-start(), calls=%async_computation.3 | async-start | bytes 589824 | tf_op jit(solution)/shard_map/reduce_scatter | solution.py:162
  46.3 1.0 copy-start.15
  46.3 1.8 copy-start.14
  46.3 2.5 copy-start.16
  47.3 33.5 %copy-start.1 = (bf16[1024,128]{1,0:T(8,128)(2,1)}, bf16[1024,128]{1,0:T(8,128)(2,1)S(1)}, u32[]{:S(2)}) copy-start(bf16[1024,128]{1,0:T(8,128)(2,1)S(1)} %get-tuple-element.813) | copy-start | bytes 786436
  47.3 33.5 %copy-start.10 = (bf16[256,128]{1,0:T(8,128)(2,1)}, bf16[256,128]{1,0:T(8,128)(2,1)S(1)}, u32[]{:S(2)}) copy-start(bf16[256,128]{1,0:T(8,128)(2,1)S(1)} %get-tuple-element.818) | copy-start | bytes 196612
  81.7 1.7 copy-start.11
  83.1 1.0 copy-start.2
  83.1 1.0 copy-start.7
  84.4 0.6 copy-start.8
  88.3 0.6 copy-start.12
  93.2 1.8 copy-start.13
  94.7 1.0 copy-start.3
  94.7 1.0 copy-start.4
  96.0 0.7 copy-start.5
  97.0 3.6 %copy-start.6 = (f32[256,128]{1,0:T(8,128)S(1)}, f32[256,128]{1,0:T(8,128)}, u32[]{:S(2)}) copy-start(f32[256,128]{1,0:T(8,128)} %get-tuple-element.240) | copy-start | bytes 393220
  97.0 3.6 %copy-start.9 = (f32[256,128]{1,0:T(8,128)S(1)}, f32[256,128]{1,0:T(8,128)}, u32[]{:S(2)}) copy-start(f32[256,128]{1,0:T(8,128)} %get-tuple-element.235) | copy-start | bytes 393220
  99.1 127.7 %reduce-scatter.6.cloned.1.call-start = ((), (), s32[]{:S(2)}) async-start(), calls=%async_computation.4 | async-start | bytes 589824 | tf_op jit(solution)/shard_map/reduce_scatter | solution.py:163
  100.5 153.0 %reduce-scatter.8.cloned.1.call-start = ((), (), s32[]{:S(2)}) async-start(), calls=%async_computation.5 | async-start | bytes 1310720 | tf_op jit(solution)/shard_map/reduce_scatter | solution.py:175
Sparse Core Ops, SparseCore 0:
  99.2 62.8 reduce-scatter.3
  165.7 60.9 reduce-scatter.5
  229.6 23.8 reduce-scatter.7
where the time goes:
time: 262 us
  waiting for transfers between devices  147 us (56%)
  blocking collectives  63.5 us (24%)
  local copies, waits for them, and re-layouts  15.8 us (6%)
  between operations  14.8 us (6%)
  matrix products  12.9 us (5%)
  other arithmetic  7.27 us (3%)
    reduce_scatter x1, waiting for transfers between devices, local(): lax.psum_scatter(value_stored, 'ctx', scatter_dimension=0, tiled=True)  62.4 us
    reduce_scatter x1, waiting for transfers between devices, local(): lax.psum_scatter(key_stored, 'ctx', scatter_dimension=0, tiled=True)  60.5 us
    all_gather x1, blocking collectives, local(): lax.all_gather(key_rows, 'ctx', axis=0, tiled=True)  32.7 us
    all_gather x1, blocking collectives, local(): lax.all_gather(value_matrix, 'ctx', axis=0, tiled=True)  30.7 us
    reduce_scatter x1, waiting for transfers between devices, local(): lax.psum_scatter(partial_sum, 'tp', scatter_dimension=1, tiled=True)  24 us
    dot_general x9, matrix products, contract_last(): lax.dot_general(left, right, (((1,), (1,)), ((), ())), preferred_element_...  10.9 us
  transfers between devices with their start and end apart: 3, of which 3 were waited for; matrix products, arithmetic and copies ran while one was open for 2% of the time, Pallas kernels for 0%

commit v1 on v0

v1 whole, which is shorter than its diff:
```python
import functools

import jax
import jax.numpy as jnp
from jax import lax
from jax.experimental import pallas as pl
from jax.experimental.pallas import tpu as pltpu
from jax.sharding import PartitionSpec as P

HEAD_SIZE = 128
PAIR = 2
SCORE_SCALE = HEAD_SIZE ** (-0.5)
LOG2_E = 1.4426950408889634
MESH = pl.DeviceIdType.MESH


def nt_dot(left, right):
    return lax.dot_general(
        left, right, (((1,), (1,)), ((), ())), preferred_element_type=jnp.float32
    )


def nn_dot(left, right):
    return lax.dot_general(
        left, right, (((1,), (0,)), ((), ())), preferred_element_type=jnp.float32
    )


def tn_dot(left, right):
    return lax.dot_general(
        left, right, (((0,), (0,)), ((), ())), preferred_element_type=jnp.float32
    )


def each(count, body):
    if count <= 8:
        for index in range(count):
            body(index)
    else:
        lax.fori_loop(0, count, lambda index, _: (body(index), 0)[1], 0)


def kernel(
    ctx_size,
    tp_size,
    q_ref,
    k_ref,
    v_ref,
    o_ref,
    g_ref,
    wq_ref,
    wk_ref,
    wv_ref,
    pos_ref,
    out_ref,
    q_in,
    g_in,
    o_in,
    wq,
    wk,
    wv,
    kv,
    q_rows,
    g_rows,
    delta,
    scores,
    row_max,
    row_sum,
    dq_t,
    pair_out,
    pair_in,
    own_part,
    far_out,
    far_in,
    proj,
    tp_out,
    tp_in,
    local_sem,
    kv_send,
    kv_fwd,
    kv_recv,
    pair_send,
    pair_recv,
    far_send,
    far_recv,
    tp_send,
    tp_recv,
):
    rows = q_ref.shape[0]
    span = rows // 2
    heads = q_ref.shape[1] // HEAD_SIZE
    query_rows = heads * rows
    far_size = ctx_size // PAIR
    features = out_ref.shape[1]
    chunk = min(far_size, 4)
    chunks = far_size // chunk
    chunk_rows = chunk * rows

    c = lax.axis_index("ctx")
    t = lax.axis_index("tp")
    a = lax.div(c, PAIR)
    b = lax.rem(c, PAIR)
    partner = (a * PAIR + 1 - b, t)

    def far(step):
        return lax.rem(a + step, far_size)

    def far_device(other):
        return (other * PAIR + b, t)

    local_pairs = [
        (q_ref, q_in),
        (g_ref, g_in),
        (o_ref, o_in),
        (k_ref, kv.at[0, b, a]),
        (v_ref, kv.at[1, b, a]),
        (wq_ref, wq),
        (wk_ref, wk),
        (wv_ref, wv),
    ]
    local_copies = [
        pltpu.make_async_copy(src, dst, local_sem.at[i]) for i, (src, dst) in enumerate(local_pairs)
    ]
    for copy in local_copies:
        copy.start()

    barrier = pltpu.get_barrier_semaphore()

    def greet_far(i):
        pl.semaphore_signal(barrier, inc=1, device_id=far_device(far(i + 1)), device_id_type=MESH)

    each(far_size - 1, greet_far)
    pl.semaphore_signal(barrier, inc=1, device_id=partner, device_id_type=MESH)
    for step in range(1, tp_size):
        pl.semaphore_signal(
            barrier, inc=1, device_id=(c, lax.rem(t + step, tp_size)), device_id_type=MESH
        )
    pl.semaphore_wait(barrier, far_size - 1 + 1 + tp_size - 1)

    def direct_copy(kind, i):
        return pltpu.make_async_remote_copy(
            src_ref=(k_ref, v_ref)[kind],
            dst_ref=kv.at[kind, b, a],
            send_sem=kv_send.at[kind, i],
            recv_sem=kv_recv.at[kind, b, a],
            device_id=far_device(far(i + 1)),
            device_id_type=MESH,
        )

    def own_forward(kind):
        return pltpu.make_async_remote_copy(
            src_ref=(k_ref, v_ref)[kind],
            dst_ref=kv.at[kind, b, a],
            send_sem=kv_fwd.at[kind, a],
            recv_sem=kv_recv.at[kind, b, a],
            device_id=partner,
            device_id_type=MESH,
        )

    def forward(kind, group, other):
        return pltpu.make_async_remote_copy(
            src_ref=kv.at[kind, group, other],
            dst_ref=kv.at[kind, group, other],
            send_sem=kv_fwd.at[kind, other],
            recv_sem=kv_recv.at[kind, group, other],
            device_id=partner,
            device_id_type=MESH,
        )

    for kind in range(2):
        each(far_size - 1, lambda i, kind=kind: direct_copy(kind, i).start())
        own_forward(kind).start()

    for copy in local_copies[:3]:
        copy.wait()
    for head in range(heads):
        lanes = slice(head * HEAD_SIZE, (head + 1) * HEAD_SIZE)
        held = slice(head * rows, (head + 1) * rows)
        q_rows[held, :] = q_in[:, lanes]
        g_head = g_in[:, lanes]
        g_rows[held, :] = g_head
        products = g_head.astype(jnp.float32) * o_in[:, lanes].astype(jnp.float32)
        delta[:, held] = jnp.sum(products.T, axis=0, keepdims=True)

    lane = lax.rem(lax.broadcasted_iota(jnp.int32, (1, query_rows), 1), rows)
    query_pos = lane + jnp.where(
        lane < span, pos_ref[PAIR * c] * span, pos_ref[PAIR * c + 1] * span - span
    )
    key_offset = lax.broadcasted_iota(jnp.int32, (span, 1), 0)

    row_max[...] = jnp.full_like(row_max, -jnp.inf)
    row_sum[...] = jnp.zeros_like(row_sum)
    dq_t[...] = jnp.zeros_like(dq_t)

    def block_start(index):
        return index * chunk_rows if isinstance(index, int) else pl.multiple_of(index * chunk_rows, chunk_rows)

    def score_chunk(which, group, index):
        first = index * chunk
        keys = kv[0, group, pl.ds(first, chunk)].reshape(chunk_rows, HEAD_SIZE)
        raw = nt_dot(keys, q_rows[...]) * (SCORE_SCALE * LOG2_E)
        best = row_max[...]
        for part in range(2 * chunk):
            stored = 2 * ((first + part // 2) * PAIR + group) + part % 2
            key_pos = pos_ref[stored] * span + key_offset
            masked = jnp.where(
                key_pos <= query_pos, raw[part * span : (part + 1) * span], -jnp.inf
            )
            scores[which, pl.ds(block_start(index) + part * span, span), :] = masked
            best = jnp.maximum(best, jnp.max(masked, axis=0, keepdims=True))
        row_max[...] = best

    def exp_chunk(which, index):
        at = pl.ds(block_start(index), chunk_rows)
        weights = jnp.exp2(scores[which, at, :] - row_max[...])
        scores[which, at, :] = weights
        row_sum[...] += jnp.sum(weights, axis=0, keepdims=True)

    def grad_chunk(which, group, index, inverse_sum):
        first = index * chunk
        keys = kv[0, group, pl.ds(first, chunk)].reshape(chunk_rows, HEAD_SIZE)
        values = kv[1, group, pl.ds(first, chunk)].reshape(chunk_rows, HEAD_SIZE)
        probs = scores[which, pl.ds(block_start(index), chunk_rows), :] * inverse_sum
        grad_probs = nt_dot(values, g_rows[...])
        grad_scores = (probs * (grad_probs - delta[...])).astype(jnp.bfloat16)
        part_value = nn_dot(probs.astype(jnp.bfloat16), g_rows[...])
        part_key = nn_dot(grad_scores, q_rows[...]) * SCORE_SCALE
        dq_t[...] += tn_dot(keys, grad_scores)
        target = pair_out if which == 1 else own_part
        target[pl.ds(first, chunk), 0] = part_key.reshape(chunk, rows, HEAD_SIZE).astype(target.dtype)
        target[pl.ds(first, chunk), 1] = part_value.reshape(chunk, rows, HEAD_SIZE).astype(target.dtype)

    def pass_on(kind):
        def one(i):
            other = far(i + 1)
            forward(kind, b, other).wait_recv()
            forward(kind, b, other).start()

        each(far_size - 1, one)

    def await_pair(kind):
        each(far_size, lambda i: forward(kind, 1 - b, i).wait_recv())

    pass_on(0)
    local_copies[3].wait()
    each(chunks, lambda i: score_chunk(0, b, i))
    pass_on(1)
    local_copies[4].wait()
    await_pair(0)
    each(chunks, lambda i: score_chunk(1, 1 - b, i))
    each(chunks, lambda i: exp_chunk(1, i))
    each(chunks, lambda i: exp_chunk(0, i))
    inverse_sum = 1.0 / row_sum[...]
    await_pair(1)
    each(chunks, lambda i: grad_chunk(1, 1 - b, i, inverse_sum))

    def pair_copy(other):
        return pltpu.make_async_remote_copy(
            src_ref=pair_out.at[other],
            dst_ref=pair_in.at[other],
            send_sem=pair_send.at[other],
            recv_sem=pair_recv.at[other],
            device_id=partner,
            device_id_type=MESH,
        )

    def far_copy(i):
        return pltpu.make_async_remote_copy(
            src_ref=far_out.at[i],
            dst_ref=far_in.at[i],
            send_sem=far_send.at[i],
            recv_sem=far_recv.at[i],
            device_id=far_device(far(i + 1)),
            device_id_type=MESH,
        )

    each(far_size, lambda i: pair_copy(far(i + 1)).start())
    each(chunks, lambda i: grad_chunk(0, b, i, inverse_sum))

    def send_far(i):
        other = far(i + 1)
        pair_copy(other).wait_recv()
        far_out[i] = (own_part[other] + pair_in[other].astype(jnp.float32)).astype(jnp.bfloat16)
        far_copy(i).start()

    each(far_size - 1, send_far)

    for copy in local_copies[5:]:
        copy.wait()
    grad_query = (dq_t[...] * SCORE_SCALE).astype(jnp.bfloat16)
    stacked = jnp.concatenate(
        [grad_query[:, head * rows : (head + 1) * rows] for head in range(heads)], axis=0
    )
    proj[...] = nn_dot(wq[...], stacked)

    pair_copy(a).wait_recv()
    own_part[a] += pair_in[a].astype(jnp.float32)

    def add_far(i):
        far_copy(i).wait_recv()
        own_part[a] += far_in[i].astype(jnp.float32)

    each(far_size - 1, add_far)
    grad_key = own_part[a, 0].astype(jnp.bfloat16)
    grad_value = own_part[a, 1].astype(jnp.bfloat16)

    def feature_block(owner):
        at = pl.ds(pl.multiple_of(owner * features, features), features)
        return proj[at, :] + nt_dot(wk[at, :], grad_key) + nt_dot(wv[at, :], grad_value)

    def tp_copy(step):
        return pltpu.make_async_remote_copy(
            src_ref=tp_out.at[step - 1],
            dst_ref=tp_in.at[step - 1],
            send_sem=tp_send.at[step - 1],
            recv_sem=tp_recv.at[step - 1],
            device_id=(c, lax.rem(t + step, tp_size)),
            device_id_type=MESH,
        )

    order = sorted(range(1, tp_size), key=lambda step: abs(step - tp_size // 2))
    for step in order:
        tp_out[step - 1] = feature_block(lax.rem(t + step, tp_size)).astype(jnp.bfloat16)
        tp_copy(step).start()
    total = feature_block(t)
    for step in reversed(order):
        tp_copy(step).wait_recv()
        total += tp_in[step - 1].astype(jnp.float32)
    out_ref[...] = total.T.astype(out_ref.dtype)

    for kind in range(2):
        each(far_size - 1, lambda i, kind=kind: direct_copy(kind, i).wait_send())
        each(far_size, lambda i, kind=kind: forward(kind, b, i).wait_send())
    each(far_size, lambda i: pair_copy(i).wait_send())
    each(far_size - 1, lambda i: far_copy(i).wait_send())
    for step in order:
        tp_copy(step).wait_send()


def local(ctx_size, tp_size, queries, key_rows, value_matrix, attention_out, output_grad, w_query, key_weight, value_weight, span_pos):
    rows, width = queries.shape
    model = w_query.shape[0]
    query_rows = rows * (width // HEAD_SIZE)
    far_size = ctx_size // PAIR
    features = model // tp_size
    block = (rows, HEAD_SIZE)
    low, full = jnp.bfloat16, jnp.float32
    dma = pltpu.SemaphoreType.DMA
    anywhere = pl.BlockSpec(memory_space=pl.ANY)
    return pl.pallas_call(
        functools.partial(kernel, ctx_size, tp_size),
        out_shape=jax.ShapeDtypeStruct((rows, features), low),
        in_specs=[anywhere] * 8 + [pl.BlockSpec(memory_space=pltpu.SMEM)],
        out_specs=pl.BlockSpec(memory_space=pltpu.VMEM),
        scratch_shapes=[
            pltpu.VMEM((rows, width), low),
            pltpu.VMEM((rows, width), low),
            pltpu.VMEM((rows, width), low),
            pltpu.VMEM(w_query.shape, low),
            pltpu.VMEM(key_weight.shape, low),
            pltpu.VMEM(value_weight.shape, low),
            pltpu.VMEM((2, PAIR, far_size) + block, low),
            pltpu.VMEM((query_rows, HEAD_SIZE), low),
            pltpu.VMEM((query_rows, HEAD_SIZE), low),
            pltpu.VMEM((1, query_rows), full),
            pltpu.VMEM((PAIR, far_size * rows, query_rows), full),
            pltpu.VMEM((1, query_rows), full),
            pltpu.VMEM((1, query_rows), full),
            pltpu.VMEM((HEAD_SIZE, query_rows), full),
            pltpu.VMEM((far_size, 2) + block, low),
            pltpu.VMEM((far_size, 2) + block, low),
            pltpu.VMEM((far_size, 2) + block, full),
            pltpu.VMEM((far_size - 1, 2) + block, low),
            pltpu.VMEM((far_size - 1, 2) + block, low),
            pltpu.VMEM((model, rows), full),
            pltpu.VMEM((tp_size - 1, features, rows), low),
            pltpu.VMEM((tp_size - 1, features, rows), low),
            dma((8,)),
            dma((2, far_size - 1)),
            dma((2, far_size)),
            dma((2, PAIR, far_size)),
            dma((far_size,)),
            dma((far_size,)),
            dma((far_size - 1,)),
            dma((far_size - 1,)),
            dma((tp_size - 1,)),
            dma((tp_size - 1,)),
        ],
        compiler_params=pltpu.CompilerParams(
            collective_id=0, has_side_effects=True, vmem_limit_bytes=52 * 1024 * 1024
        ),
    )(queries, key_rows, value_matrix, attention_out, output_grad, w_query, key_weight, value_weight, span_pos)


def solution(mesh):
    in_specs = (
        P("ctx", "tp"),
        P("ctx", "tp"),
        P("ctx", "tp"),
        P("ctx", "tp"),
        P("ctx", "tp"),
        P(None, "tp"),
        P(None, "tp"),
        P(None, "tp"),
        P(),
    )
    body = functools.partial(local, mesh.shape["ctx"], mesh.shape["tp"])
    return jax.shard_map(body, mesh=mesh, in_specs=in_specs, out_specs=P("ctx", "tp"), check_vma=False)
```

time: 262 us -> 40.5 us (0.15)
  waiting for transfers between devices: 147 us -> 0 us
  blocking collectives: 63.5 us -> 0 us
  Pallas kernels: 0 us -> 32.2 us
  between operations: 14.8 us -> 0.02 us
  matrix products: 12.9 us -> 0 us
  local copies, waits for them, and re-layouts: 15.8 us -> 7.62 us
  other arithmetic: 7.27 us -> 0 us
    reduce_scatter x3 -> x0, waiting for transfers between devices: 147 us -> none  [the longest x1 62.4 us: local(): lax.psum_scatter(value_stored, 'ctx', scatter_dimension=0, tiled=True)]
    all_gather x2 -> x0, blocking collectives: 63.5 us -> none  [the longest x1 32.7 us: local(): lax.all_gather(key_rows, 'ctx', axis=0, tiled=True)]
    pallas_call x0 -> x1, Pallas kernels: none -> 32.2 us  [local(): pl.pallas_call(functools.partial(kernel, ctx_size, tp_size), out_shape=ja...]
    dot_general x15 -> x0, matrix products: 12.9 us -> none  [the longest x9 10.9 us: contract_last(): lax.dot_general(left, right, (((1,), (1,)), ((), ())), preferred_element_...]
    unnamed x18 -> x17, local copies, waits for them, and re-layouts: 0.66 us -> 7.62 us
    gather x4 -> x0, local copies, waits for them, and re-layouts: 3.95 us -> none  [the longest x1 1.38 us: local(): value_acc.reshape(span_total, span_len, HEAD_SIZE)[span_pos]]
    slice x3 -> x0, local copies, waits for them, and re-layouts: 2.81 us -> none  [the longest x1 1.51 us: local(): queries[low:low + span_len].reshape(query_count, HEAD_SIZE)]
  transfers between devices with their start and end apart: 3 -> 0, of which waited for: 3 -> 0; matrix products, arithmetic and copies ran while one was open for 2% -> 0% of each run, Pallas kernels for 0% -> 0%
where the time goes in v1:
time: 40.5 us; the launch traced here: 39.8 us
  Pallas kernels  32.2 us (80%)
  local copies, waits for them, and re-layouts  7.62 us (19%)
    pallas_call x1, Pallas kernels, local(): pl.pallas_call(functools.partial(kernel, ctx_size, tp_size), out_shape=ja...  32.2 us
    unnamed x17, local copies, waits for them, and re-layouts  7.62 us

profile of v1, /device:TPU:0, one launch (start us, length us, event | category | flops | bytes accessed | tf_op | source)
XLA Modules:
  0.0 39.8 jit_solution(4455206924414426050)
XLA Ops:
  0.0 0.0 copy-start
  0.0 1.0 %copy-done = bf16[2048,128]{1,0:T(8,128)(2,1)S(1)} copy-done((bf16[2048,128]{1,0:T(8,128)(2,1)S(1)}, bf16[2048,128]{1,0:T(8,128)(2,1)}, u32[]{:S(2)}) %copy-start) | copy-done | bytes 524312
  1.0 0.0 copy-start.1
  1.0 1.0 %copy-done.1 = bf16[2048,128]{1,0:T(8,128)(2,1)S(1)} copy-done((bf16[2048,128]{1,0:T(8,128)(2,1)S(1)}, bf16[2048,128]{1,0:T(8,128)(2,1)}, u32[]{:S(2)}) %copy-start.1) | copy-done | bytes 524312
  2.1 0.0 copy-start.2
  2.1 0.9 %copy-done.2 = bf16[128,512]{1,0:T(8,128)(2,1)S(1)} copy-done((bf16[128,512]{1,0:T(8,128)(2,1)S(1)}, bf16[128,512]{1,0:T(8,128)(2,1)}, u32[]{:S(2)}) %copy-start.2) | copy-done | bytes 131096
  3.0 0.0 copy-start.3
  3.0 0.9 %copy-done.3 = bf16[128,512]{1,0:T(8,128)(2,1)S(1)} copy-done((bf16[128,512]{1,0:T(8,128)(2,1)S(1)}, bf16[128,512]{1,0:T(8,128)(2,1)}, u32[]{:S(2)}) %copy-start.3) | copy-done | bytes 131096
  3.9 0.0 copy-start.4
  3.9 0.9 %copy-done.4 = bf16[128,512]{1,0:T(8,128)(2,1)S(1)} copy-done((bf16[128,512]{1,0:T(8,128)(2,1)S(1)}, bf16[128,512]{1,0:T(8,128)(2,1)}, u32[]{:S(2)}) %copy-start.4) | copy-done | bytes 131096
  4.8 0.0 copy-start.5
  4.8 0.8 %copy-done.5 = bf16[128,128]{1,0:T(8,128)(2,1)S(1)} copy-done((bf16[128,128]{1,0:T(8,128)(2,1)S(1)}, bf16[128,128]{1,0:T(8,128)(2,1)}, u32[]{:S(2)}) %copy-start.5) | copy-done | bytes 32792
  5.6 0.0 copy-start.6
  5.6 0.8 %copy-done.6 = bf16[128,128]{1,0:T(8,128)(2,1)S(1)} copy-done((bf16[128,128]{1,0:T(8,128)(2,1)S(1)}, bf16[128,128]{1,0:T(8,128)(2,1)}, u32[]{:S(2)}) %copy-start.6) | copy-done | bytes 32792
  6.3 0.0 copy-start.7
  6.3 0.7 %copy-done.7 = s32[16]{0:T(128)S(1)} copy-done((s32[16]{0:T(128)S(1)}, s32[16]{0:T(128)}, u32[]{:S(2)}) %copy-start.7) | copy-done | bytes 88
  7.0 32.2 %shard_map.91 = bf16[128,512]{1,0:T(8,128)(2,1)S(1)} custom-call(bf16[128,512]{1,0:T(8,128)(2,1)S(1)} %copy-done.2, bf16[128,128]{1,0:T(8,128)(2,1)S(1)} %copy-done.5, bf16[128,128]{1,0:T(8,128)(2,1)S(1)} %copy-done.6, bf16[128,512]{1,0:T(8,128)(2,1)S(1)} %copy-done.3, bf16[128,512]{1,0:T(8,128)(2,1)S(1)} %copy-done.4, bf16[2048,512]{1,0:T(8,128)(2,1)} %wq_ref.1, ...), custom_call_target="tpu_custom_call" | custom-call | tf_op jit(solution)/shard_map/pallas_call | solution.py:350
  39.1 0.7 %copy.11 = bf16[128,512]{1,0:T(8,128)(2,1)} copy(bf16[128,512]{1,0:T(8,128)(2,1)S(1)} %shard_map.91) | data formatting | bytes 262144
Async XLA Ops:
  0.0 1.0 %copy-start = (bf16[2048,128]{1,0:T(8,128)(2,1)S(1)}, bf16[2048,128]{1,0:T(8,128)(2,1)}, u32[]{:S(2)}) copy-start(bf16[2048,128]{1,0:T(8,128)(2,1)} %wk_ref.1) | copy-start | bytes 1572868
  1.0 1.0 %copy-start.1 = (bf16[2048,128]{1,0:T(8,128)(2,1)S(1)}, bf16[2048,128]{1,0:T(8,128)(2,1)}, u32[]{:S(2)}) copy-start(bf16[2048,128]{1,0:T(8,128)(2,1)} %wv_ref.1) | copy-start | bytes 1572868
  2.1 0.9 %copy-start.2 = (bf16[128,512]{1,0:T(8,128)(2,1)S(1)}, bf16[128,512]{1,0:T(8,128)(2,1)}, u32[]{:S(2)}) copy-start(bf16[128,512]{1,0:T(8,128)(2,1)} %q_ref.1) | copy-start | bytes 393220
  3.0 0.9 %copy-start.3 = (bf16[128,512]{1,0:T(8,128)(2,1)S(1)}, bf16[128,512]{1,0:T(8,128)(2,1)}, u32[]{:S(2)}) copy-start(bf16[128,512]{1,0:T(8,128)(2,1)} %o_ref.1) | copy-start | bytes 393220
  3.9 0.9 %copy-start.4 = (bf16[128,512]{1,0:T(8,128)(2,1)S(1)}, bf16[128,512]{1,0:T(8,128)(2,1)}, u32[]{:S(2)}) copy-start(bf16[128,512]{1,0:T(8,128)(2,1)} %g_ref.1) | copy-start | bytes 393220
  4.8 0.8 %copy-start.5 = (bf16[128,128]{1,0:T(8,128)(2,1)S(1)}, bf16[128,128]{1,0:T(8,128)(2,1)}, u32[]{:S(2)}) copy-start(bf16[128,128]{1,0:T(8,128)(2,1)} %k_ref.1) | copy-start | bytes 98308
  5.6 0.8 %copy-start.6 = (bf16[128,128]{1,0:T(8,128)(2,1)S(1)}, bf16[128,128]{1,0:T(8,128)(2,1)}, u32[]{:S(2)}) copy-start(bf16[128,128]{1,0:T(8,128)(2,1)} %v_ref.1) | copy-start | bytes 98308
  6.3 0.7 %copy-start.7 = (s32[16]{0:T(128)S(1)}, s32[16]{0:T(128)}, u32[]{:S(2)}) copy-start(s32[16]{0:T(128)} %pos_ref.1) | copy-start | bytes 196

commit v2 on v1

--- a/solution.py
+++ b/solution.py
@@ -57,8 +57,7 @@
     g_in,
     o_in,
     wq,
-    wk,
-    wv,
+    w_kv,
     kv,
     q_rows,
     g_rows,
@@ -72,7 +71,6 @@
     own_part,
     far_out,
     far_in,
-    proj,
     tp_out,
     tp_in,
     local_sem,
@@ -85,6 +83,11 @@
     far_recv,
     tp_send,
     tp_recv,
+    g_kv,
+    w_send,
+    w_recv,
+    g_send,
+    g_recv,
 ):
     rows = q_ref.shape[0]
     span = rows // 2
@@ -108,6 +111,15 @@
     def far_device(other):
         return (other * PAIR + b, t)
 
+    def feature_rows(owner):
+        return pl.ds(pl.multiple_of(owner * features, features), features)
+
+    def tp_peer(step):
+        return lax.rem(t + step, tp_size)
+
+    own_features = feature_rows(t)
+    order = sorted(range(1, tp_size), key=lambda step: abs(step - tp_size // 2))
+
     local_pairs = [
         (q_ref, q_in),
         (g_ref, g_in),
@@ -115,8 +127,8 @@
         (k_ref, kv.at[0, b, a]),
         (v_ref, kv.at[1, b, a]),
         (wq_ref, wq),
-        (wk_ref, wk),
-        (wv_ref, wv),
+        (wk_ref.at[own_features], w_kv.at[t, 0]),
+        (wv_ref.at[own_features], w_kv.at[t, 1]),
     ]
     local_copies = [
         pltpu.make_async_copy(src, dst, local_sem.at[i]) for i, (src, dst) in enumerate(local_pairs)
@@ -170,6 +182,20 @@
     for kind in range(2):
         each(far_size - 1, lambda i, kind=kind: direct_copy(kind, i).start())
         own_forward(kind).start()
+
+    def weight_copy(step, kind):
+        return pltpu.make_async_remote_copy(
+            src_ref=(wk_ref, wv_ref)[kind].at[feature_rows(tp_peer(step))],
+            dst_ref=w_kv.at[t, kind],
+            send_sem=w_send.at[step - 1, kind],
+            recv_sem=w_recv.at[step - 1, kind],
+            device_id=(c, tp_peer(step)),
+            device_id_type=MESH,
+        )
+
+    for kind in (1, 0):
+        for step in order:
+            weight_copy(step, kind).start()
 
     for copy in local_copies[:3]:
         copy.wait()
@@ -216,19 +242,25 @@
         scores[which, at, :] = weights
         row_sum[...] += jnp.sum(weights, axis=0, keepdims=True)
 
-    def grad_chunk(which, group, index, inverse_sum):
+    def store_part(which, kind, first, part):
+        target = pair_out if which == 1 else own_part
+        target[kind, pl.ds(first, chunk)] = part.reshape(chunk, rows, HEAD_SIZE).astype(target.dtype)
+
+    def value_chunk(which, index, inverse_sum):
+        at = pl.ds(block_start(index), chunk_rows)
+        probs = scores[which, at, :] * inverse_sum
+        scores[which, at, :] = probs
+        store_part(which, 1, index * chunk, nn_dot(probs.astype(jnp.bfloat16), g_rows[...]))
+
+    def key_chunk(which, group, index):
         first = index * chunk
         keys = kv[0, group, pl.ds(first, chunk)].reshape(chunk_rows, HEAD_SIZE)
         values = kv[1, group, pl.ds(first, chunk)].reshape(chunk_rows, HEAD_SIZE)
-        probs = scores[which, pl.ds(block_start(index), chunk_rows), :] * inverse_sum
+        probs = scores[which, pl.ds(block_start(index), chunk_rows), :]
         grad_probs = nt_dot(values, g_rows[...])
         grad_scores = (probs * (grad_probs - delta[...])).astype(jnp.bfloat16)
-        part_value = nn_dot(probs.astype(jnp.bfloat16), g_rows[...])
-        part_key = nn_dot(grad_scores, q_rows[...]) * SCORE_SCALE
+        store_part(which, 0, first, nn_dot(grad_scores, q_rows[...]) * SCORE_SCALE)
         dq_t[...] += tn_dot(keys, grad_scores)
-        target = pair_out if which == 1 else own_part
-        target[pl.ds(first, chunk), 0] = part_key.reshape(chunk, rows, HEAD_SIZE).astype(target.dtype)
-        target[pl.ds(first, chunk), 1] = part_value.reshape(chunk, rows, HEAD_SIZE).astype(target.dtype)
 
     def pass_on(kind):
         def one(i):
@@ -251,62 +283,49 @@
     each(chunks, lambda i: exp_chunk(1, i))
     each(chunks, lambda i: exp_chunk(0, i))
     inverse_sum = 1.0 / row_sum[...]
+
+    def pair_copy(kind, other):
+        return pltpu.make_async_remote_copy(
+            src_ref=pair_out.at[kind, other],
+            dst_ref=pair_in.at[kind, other],
+            send_sem=pair_send.at[kind, other],
+            recv_sem=pair_recv.at[kind, other],
+            device_id=partner,
+            device_id_type=MESH,
+        )
+
+    def far_copy(kind, i):
+        return pltpu.make_async_remote_copy(
+            src_ref=far_out.at[kind, i],
+            dst_ref=far_in.at[kind, i],
+            send_sem=far_send.at[kind, i],
+            recv_sem=far_recv.at[kind, i],
+            device_id=far_device(far(i + 1)),
+            device_id_type=MESH,
+        )
+
+    def send_far(kind, i):
+        other = far(i + 1)
+        pair_copy(kind, other).wait_recv()
+        far_out[kind, i] = (
+            own_part[kind, other] + pair_in[kind, other].astype(jnp.float32)
+        ).astype(jnp.bfloat16)
+        far_copy(kind, i).start()
+
+    each(chunks, lambda i: value_chunk(1, i, inverse_sum))
+    each(far_size, lambda i: pair_copy(1, far(i + 1)).start())
+    each(chunks, lambda i: value_chunk(0, i, inverse_sum))
     await_pair(1)
-    each(chunks, lambda i: grad_chunk(1, 1 - b, i, inverse_sum))
-
-    def pair_copy(other):
-        return pltpu.make_async_remote_copy(
-            src_ref=pair_out.at[other],
-            dst_ref=pair_in.at[other],
-            send_sem=pair_send.at[other],
-            recv_sem=pair_recv.at[other],
-            device_id=partner,
-            device_id_type=MESH,
-        )
-
-    def far_copy(i):
-        return pltpu.make_async_remote_copy(
-            src_ref=far_out.at[i],
-            dst_ref=far_in.at[i],
-            send_sem=far_send.at[i],
-            recv_sem=far_recv.at[i],
-            device_id=far_device(far(i + 1)),
-            device_id_type=MESH,
-        )
-
-    each(far_size, lambda i: pair_copy(far(i + 1)).start())
-    each(chunks, lambda i: grad_chunk(0, b, i, inverse_sum))
-
-    def send_far(i):
-        other = far(i + 1)
-        pair_copy(other).wait_recv()
-        far_out[i] = (own_part[other] + pair_in[other].astype(jnp.float32)).astype(jnp.bfloat16)
-        far_copy(i).start()
-
-    each(far_size - 1, send_far)
-
-    for copy in local_copies[5:]:
-        copy.wait()
+    each(chunks, lambda i: key_chunk(1, 1 - b, i))
+    each(far_size, lambda i: pair_copy(0, far(i + 1)).start())
+    each(chunks, lambda i: key_chunk(0, b, i))
+    each(far_size - 1, lambda i: send_far(1, i))
+
+    local_copies[5].wait()
     grad_query = (dq_t[...] * SCORE_SCALE).astype(jnp.bfloat16)
     stacked = jnp.concatenate(
         [grad_query[:, head * rows : (head + 1) * rows] for head in range(heads)], axis=0
     )
-    proj[...] = nn_dot(wq[...], stacked)
-
-    pair_copy(a).wait_recv()
-    own_part[a] += pair_in[a].astype(jnp.float32)
-
-    def add_far(i):
-        far_copy(i).wait_recv()
-        own_part[a] += far_in[i].astype(jnp.float32)
-
-    each(far_size - 1, add_far)
-    grad_key = own_part[a, 0].astype(jnp.bfloat16)
-    grad_value = own_part[a, 1].astype(jnp.bfloat16)
-
-    def feature_block(owner):
-        at = pl.ds(pl.multiple_of(owner * features, features), features)
-        return proj[at, :] + nt_dot(wk[at, :], grad_key) + nt_dot(wv[at, :], grad_value)
 
     def tp_copy(step):
         return pltpu.make_async_remote_copy(
@@ -314,25 +333,62 @@
             dst_ref=tp_in.at[step - 1],
             send_sem=tp_send.at[step - 1],
             recv_sem=tp_recv.at[step - 1],
-            device_id=(c, lax.rem(t + step, tp_size)),
-            device_id_type=MESH,
-        )
-
-    order = sorted(range(1, tp_size), key=lambda step: abs(step - tp_size // 2))
+            device_id=(c, tp_peer(step)),
+            device_id_type=MESH,
+        )
+
     for step in order:
-        tp_out[step - 1] = feature_block(lax.rem(t + step, tp_size)).astype(jnp.bfloat16)
+        tp_out[step - 1] = nn_dot(wq[feature_rows(tp_peer(step)), :], stacked).astype(jnp.bfloat16)
         tp_copy(step).start()
-    total = feature_block(t)
+    each(far_size - 1, lambda i: send_far(0, i))
+    own_proj = nn_dot(wq[own_features, :], stacked)
+
+    def grad_copy(step, kind):
+        return pltpu.make_async_remote_copy(
+            src_ref=g_kv.at[t, kind],
+            dst_ref=g_kv.at[t, kind],
+            send_sem=g_send.at[step - 1, kind],
+            recv_sem=g_recv.at[step - 1, kind],
+            device_id=(c, tp_peer(step)),
+            device_id_type=MESH,
+        )
+
+    def add_far(kind, i):
+        far_copy(kind, i).wait_recv()
+        own_part[kind, a] += far_in[kind, i].astype(jnp.float32)
+
+    def finish(kind):
+        pair_copy(kind, a).wait_recv()
+        own_part[kind, a] += pair_in[kind, a].astype(jnp.float32)
+        each(far_size - 1, lambda i: add_far(kind, i))
+        g_kv[t, kind] = own_part[kind, a].astype(jnp.bfloat16)
+        for step in order:
+            grad_copy(step, kind).start()
+
+    finish(1)
     for step in reversed(order):
         tp_copy(step).wait_recv()
-        total += tp_in[step - 1].astype(jnp.float32)
-    out_ref[...] = total.T.astype(out_ref.dtype)
+        own_proj += tp_in[step - 1].astype(jnp.float32)
+    total = own_proj.T
+    finish(0)
+    for kind in (1, 0):
+        local_copies[6 + kind].wait()
+        total += nt_dot(g_kv[t, kind], w_kv[t, kind])
+        for step in reversed(order):
+            sender = lax.rem(t + tp_size - step, tp_size)
+            weight_copy(step, kind).wait_recv()
+            grad_copy(step, kind).wait_recv()
+            total += nt_dot(g_kv[sender, kind], w_kv[sender, kind])
+    out_ref[...] = total.astype(out_ref.dtype)
 
     for kind in range(2):
         each(far_size - 1, lambda i, kind=kind: direct_copy(kind, i).wait_send())
         each(far_size, lambda i, kind=kind: forward(kind, b, i).wait_send())
-    each(far_size, lambda i: pair_copy(i).wait_send())
-    each(far_size - 1, lambda i: far_copy(i).wait_send())
+        each(far_size, lambda i, kind=kind: pair_copy(kind, i).wait_send())
+        each(far_size - 1, lambda i, kind=kind: far_copy(kind, i).wait_send())
+        for step in order:
+            weight_copy(step, kind).wait_send()
+            grad_copy(step, kind).wait_send()
     for step in order:
         tp_copy(step).wait_send()
 
@@ -346,19 +402,18 @@
     block = (rows, HEAD_SIZE)
     low, full = jnp.bfloat16, jnp.float32
     dma = pltpu.SemaphoreType.DMA
-    anywhere = pl.BlockSpec(memory_space=pl.ANY)
+    in_hbm = pl.BlockSpec(memory_space=pltpu.HBM)
     return pl.pallas_call(
         functools.partial(kernel, ctx_size, tp_size),
         out_shape=jax.ShapeDtypeStruct((rows, features), low),
-        in_specs=[anywhere] * 8 + [pl.BlockSpec(memory_space=pltpu.SMEM)],
+        in_specs=[in_hbm] * 8 + [pl.BlockSpec(memory_space=pltpu.SMEM)],
         out_specs=pl.BlockSpec(memory_space=pltpu.VMEM),
         scratch_shapes=[
             pltpu.VMEM((rows, width), low),
             pltpu.VMEM((rows, width), low),
             pltpu.VMEM((rows, width), low),
             pltpu.VMEM(w_query.shape, low),
-            pltpu.VMEM(key_weight.shape, low),
-            pltpu.VMEM(value_weight.shape, low),
+            pltpu.VMEM((tp_size, 2, features, HEAD_SIZE), low),
             pltpu.VMEM((2, PAIR, far_size) + block, low),
             pltpu.VMEM((query_rows, HEAD_SIZE), low),
             pltpu.VMEM((query_rows, HEAD_SIZE), low),
@@ -367,27 +422,31 @@
             pltpu.VMEM((1, query_rows), full),
             pltpu.VMEM((1, query_rows), full),
             pltpu.VMEM((HEAD_SIZE, query_rows), full),
-            pltpu.VMEM((far_size, 2) + block, low),
-            pltpu.VMEM((far_size, 2) + block, low),
-            pltpu.VMEM((far_size, 2) + block, full),
-            pltpu.VMEM((far_size - 1, 2) + block, low),
-            pltpu.VMEM((far_size - 1, 2) + block, low),
-            pltpu.VMEM((model, rows), full),
+            pltpu.VMEM((2, far_size) + block, low),
+            pltpu.VMEM((2, far_size) + block, low),
+            pltpu.VMEM((2, far_size) + block, full),
+            pltpu.VMEM((2, far_size - 1) + block, low),
+            pltpu.VMEM((2, far_size - 1) + block, low),
             pltpu.VMEM((tp_size - 1, features, rows), low),
             pltpu.VMEM((tp_size - 1, features, rows), low),
             dma((8,)),
             dma((2, far_size - 1)),
             dma((2, far_size)),
             dma((2, PAIR, far_size)),
-            dma((far_size,)),
-            dma((far_size,)),
-            dma((far_size - 1,)),
-            dma((far_size - 1,)),
+            dma((2, far_size)),
+            dma((2, far_size)),
+            dma((2, far_size - 1)),
+            dma((2, far_size - 1)),
             dma((tp_size - 1,)),
             dma((tp_size - 1,)),
+            pltpu.VMEM((tp_size, 2) + block, low),
+            dma((tp_size - 1, 2)),
+            dma((tp_size - 1, 2)),
+            dma((tp_size - 1, 2)),
+            dma((tp_size - 1, 2)),
         ],
         compiler_params=pltpu.CompilerParams(
-            collective_id=0, has_side_effects=True, vmem_limit_bytes=52 * 1024 * 1024
+            collective_id=0, has_side_effects=True, vmem_limit_bytes=63 * 1024 * 1024
         ),
     )(queries, key_rows, value_matrix, attention_out, output_grad, w_query, key_weight, value_weight, span_pos)
 

time: 40.5 us -> 32.8 us (0.81); the launches traced: 39.8 us -> 32.6 us
  local copies, waits for them, and re-layouts: 7.62 us -> 1.57 us
  Pallas kernels: 32.2 us -> 31.1 us
    unnamed x17 -> x1, local copies, waits for them, and re-layouts: 7.62 us -> 1.57 us
    pallas_call x1, Pallas kernels: 32.2 us -> 31.1 us  [local(): pl.pallas_call(functools.partial(kernel, ctx_size, tp_size), out_shape=ja...]
where the time goes in v2:
time: 32.8 us; the launch traced here: 32.6 us
  Pallas kernels  31.1 us (95%)
  local copies, waits for them, and re-layouts  1.57 us (5%)
    pallas_call x1, Pallas kernels, local(): pl.pallas_call(functools.partial(kernel, ctx_size, tp_size), out_shape=ja...  31.1 us
    unnamed x1, local copies, waits for them, and re-layouts  1.57 us

profile of v2, /device:TPU:0, one launch (start us, length us, event | category | flops | bytes accessed | tf_op | source)
XLA Modules:
  0.0 32.6 jit_solution(7796517848965806026)
XLA Ops:
  0.0 31.1 %shard_map.91 = bf16[128,512]{1,0:T(8,128)(2,1)} custom-call(bf16[128,512]{1,0:T(8,128)(2,1)} %q_ref.1, bf16[128,128]{1,0:T(8,128)(2,1)} %k_ref.1, bf16[128,128]{1,0:T(8,128)(2,1)} %v_ref.1, bf16[128,512]{1,0:T(8,128)(2,1)} %o_ref.1, bf16[128,512]{1,0:T(8,128)(2,1)} %g_ref.1, bf16[2048,512]{1,0:T(8,128)(2,1)} %wq_ref.1, bf16[2048,128]{1,0:T(8,128)(2,1)} %wk_ref.1, ...), custom_call_target="tpu_custom_call" | custom-call | tf_op jit(solution)/shard_map/pallas_call | solution.py:406
  31.1 1.6 %copy.11 = bf16[128,512]{1,0:T(8,128)(2,1)} copy(bf16[128,512]{1,0:T(8,128)(2,1)} %shard_map.91) | data formatting | bytes 262144

commit v3 on v2

--- a/solution.py
+++ b/solution.py
@@ -63,6 +63,7 @@
     g_rows,
     delta,
     scores,
+    grad_scores,
     row_max,
     row_sum,
     dq_t,
@@ -218,71 +219,69 @@
     row_sum[...] = jnp.zeros_like(row_sum)
     dq_t[...] = jnp.zeros_like(dq_t)
 
-    def block_start(index):
-        return index * chunk_rows if isinstance(index, int) else pl.multiple_of(index * chunk_rows, chunk_rows)
-
-    def score_chunk(which, group, index):
-        first = index * chunk
-        keys = kv[0, group, pl.ds(first, chunk)].reshape(chunk_rows, HEAD_SIZE)
-        raw = nt_dot(keys, q_rows[...]) * (SCORE_SCALE * LOG2_E)
-        best = row_max[...]
-        for part in range(2 * chunk):
-            stored = 2 * ((first + part // 2) * PAIR + group) + part % 2
-            key_pos = pos_ref[stored] * span + key_offset
-            masked = jnp.where(
-                key_pos <= query_pos, raw[part * span : (part + 1) * span], -jnp.inf
-            )
-            scores[which, pl.ds(block_start(index) + part * span, span), :] = masked
+    def score_block(which, group, other):
+        raw = nt_dot(kv[0, group, other], q_rows[...]) * (SCORE_SCALE * LOG2_E)
+        best = row_max[which]
+        for part in range(2):
+            key_pos = pos_ref[2 * (other * PAIR + group) + part] * span + key_offset
+            masked = jnp.where(key_pos <= query_pos, raw[part * span : (part + 1) * span], -jnp.inf)
+            scores[which, other, part * span : (part + 1) * span, :] = masked
             best = jnp.maximum(best, jnp.max(masked, axis=0, keepdims=True))
-        row_max[...] = best
-
-    def exp_chunk(which, index):
-        at = pl.ds(block_start(index), chunk_rows)
-        weights = jnp.exp2(scores[which, at, :] - row_max[...])
-        scores[which, at, :] = weights
-        row_sum[...] += jnp.sum(weights, axis=0, keepdims=True)
-
-    def store_part(which, kind, first, part):
+        row_max[which] = best
+
+    def exp_block(which, other):
+        weights = jnp.exp2(scores[which, other] - row_max[which])
+        scores[which, other] = weights
+        row_sum[which] += jnp.sum(weights, axis=0, keepdims=True)
+
+    def value_block(which, other, factor):
+        probs = scores[which, other] * factor
+        scores[which, other] = probs
+        part = nn_dot(probs.astype(jnp.bfloat16), g_rows[...])
         target = pair_out if which == 1 else own_part
-        target[kind, pl.ds(first, chunk)] = part.reshape(chunk, rows, HEAD_SIZE).astype(target.dtype)
-
-    def value_chunk(which, index, inverse_sum):
-        at = pl.ds(block_start(index), chunk_rows)
-        probs = scores[which, at, :] * inverse_sum
-        scores[which, at, :] = probs
-        store_part(which, 1, index * chunk, nn_dot(probs.astype(jnp.bfloat16), g_rows[...]))
-
-    def key_chunk(which, group, index):
-        first = index * chunk
-        keys = kv[0, group, pl.ds(first, chunk)].reshape(chunk_rows, HEAD_SIZE)
-        values = kv[1, group, pl.ds(first, chunk)].reshape(chunk_rows, HEAD_SIZE)
-        probs = scores[which, pl.ds(block_start(index), chunk_rows), :]
-        grad_probs = nt_dot(values, g_rows[...])
-        grad_scores = (probs * (grad_probs - delta[...])).astype(jnp.bfloat16)
-        store_part(which, 0, first, nn_dot(grad_scores, q_rows[...]) * SCORE_SCALE)
-        dq_t[...] += tn_dot(keys, grad_scores)
-
-    def pass_on(kind):
-        def one(i):
-            other = far(i + 1)
-            forward(kind, b, other).wait_recv()
-            forward(kind, b, other).start()
-
-        each(far_size - 1, one)
-
-    def await_pair(kind):
-        each(far_size, lambda i: forward(kind, 1 - b, i).wait_recv())
-
-    pass_on(0)
+        target[1, other] = part.astype(target.dtype)
+
+    def key_block(which, group, other):
+        grad_probs = nt_dot(kv[1, group, other], g_rows[...])
+        grads = (scores[which, other] * (grad_probs - delta[...])).astype(jnp.bfloat16)
+        grad_scores[which, other] = grads
+        part = nn_dot(grads, q_rows[...]) * SCORE_SCALE
+        target = pair_out if which == 1 else own_part
+        target[0, other] = part.astype(target.dtype)
+
+    def query_chunk(which, group, index):
+        at = pl.ds(index * chunk, chunk)
+        keys = kv[0, group, at].reshape(chunk_rows, HEAD_SIZE)
+        dq_t[...] += tn_dot(keys, grad_scores[which, at].reshape(chunk_rows, query_rows))
+
+    def key_arrival(i):
+        other = far(i + 1)
+        forward(0, b, other).wait_recv()
+        forward(0, b, other).start()
+        score_block(0, b, other)
+
+    def value_arrival(i):
+        other = far(i + 1)
+        forward(1, b, other).wait_recv()
+        forward(1, b, other).start()
+
+    def pair_key_arrival(i):
+        other = far(i)
+        forward(0, 1 - b, other).wait_recv()
+        score_block(1, 1 - b, other)
+
     local_copies[3].wait()
-    each(chunks, lambda i: score_chunk(0, b, i))
-    pass_on(1)
+    score_block(0, b, a)
+    each(far_size - 1, key_arrival)
+    each(far_size - 1, value_arrival)
+    each(far_size, lambda i: exp_block(0, i))
+    each(far_size, pair_key_arrival)
+    row_max[1] = jnp.maximum(row_max[0], row_max[1])
+    each(far_size, lambda i: exp_block(1, i))
+    own_shrink = jnp.exp2(row_max[0] - row_max[1])
+    pair_factor = 1.0 / (row_sum[0] * own_shrink + row_sum[1])
+    own_factor = own_shrink * pair_factor
     local_copies[4].wait()
-    await_pair(0)
-    each(chunks, lambda i: score_chunk(1, 1 - b, i))
-    each(chunks, lambda i: exp_chunk(1, i))
-    each(chunks, lambda i: exp_chunk(0, i))
-    inverse_sum = 1.0 / row_sum[...]
 
     def pair_copy(kind, other):
         return pltpu.make_async_remote_copy(
@@ -312,15 +311,25 @@
         ).astype(jnp.bfloat16)
         far_copy(kind, i).start()
 
-    each(chunks, lambda i: value_chunk(1, i, inverse_sum))
-    each(far_size, lambda i: pair_copy(1, far(i + 1)).start())
-    each(chunks, lambda i: value_chunk(0, i, inverse_sum))
-    await_pair(1)
-    each(chunks, lambda i: key_chunk(1, 1 - b, i))
-    each(far_size, lambda i: pair_copy(0, far(i + 1)).start())
-    each(chunks, lambda i: key_chunk(0, b, i))
+    def pair_value(i):
+        other = far(i + 1)
+        value_block(1, other, pair_factor)
+        pair_copy(1, other).start()
+
+    def pair_key(i):
+        other = far(i + 1)
+        forward(1, 1 - b, other).wait_recv()
+        key_block(1, 1 - b, other)
+        pair_copy(0, other).start()
+
+    each(far_size, pair_value)
+    each(far_size, lambda i: value_block(0, i, own_factor))
+    each(far_size, pair_key)
+    each(far_size, lambda i: key_block(0, b, i))
     each(far_size - 1, lambda i: send_far(1, i))
 
+    each(chunks, lambda i: query_chunk(1, 1 - b, i))
+    each(chunks, lambda i: query_chunk(0, b, i))
     local_copies[5].wait()
     grad_query = (dq_t[...] * SCORE_SCALE).astype(jnp.bfloat16)
     stacked = jnp.concatenate(
@@ -405,7 +414,7 @@
     in_hbm = pl.BlockSpec(memory_space=pltpu.HBM)
     return pl.pallas_call(
         functools.partial(kernel, ctx_size, tp_size),
-        out_shape=jax.ShapeDtypeStruct((rows, features), low),
+        out_shape=pltpu.VMEM((rows, features), low),
         in_specs=[in_hbm] * 8 + [pl.BlockSpec(memory_space=pltpu.SMEM)],
         out_specs=pl.BlockSpec(memory_space=pltpu.VMEM),
         scratch_shapes=[
@@ -418,9 +427,10 @@
             pltpu.VMEM((query_rows, HEAD_SIZE), low),
             pltpu.VMEM((query_rows, HEAD_SIZE), low),
             pltpu.VMEM((1, query_rows), full),
-            pltpu.VMEM((PAIR, far_size * rows, query_rows), full),
-            pltpu.VMEM((1, query_rows), full),
-            pltpu.VMEM((1, query_rows), full),
+            pltpu.VMEM((PAIR, far_size, rows, query_rows), full),
+            pltpu.VMEM((PAIR, far_size, rows, query_rows), low),
+            pltpu.VMEM((PAIR, 1, query_rows), full),
+            pltpu.VMEM((PAIR, 1, query_rows), full),
             pltpu.VMEM((HEAD_SIZE, query_rows), full),
             pltpu.VMEM((2, far_size) + block, low),
             pltpu.VMEM((2, far_size) + block, low),
@@ -446,7 +456,7 @@
             dma((tp_size - 1, 2)),
         ],
         compiler_params=pltpu.CompilerParams(
-            collective_id=0, has_side_effects=True, vmem_limit_bytes=63 * 1024 * 1024
+            collective_id=0, has_side_effects=True, vmem_limit_bytes=(65536 - 192) * 1024
         ),
     )(queries, key_rows, value_matrix, attention_out, output_grad, w_query, key_weight, value_weight, span_pos)
 

time: 32.8 us -> 31.7 us (0.966)
  local copies, waits for them, and re-layouts: 1.57 us -> 0.66 us
    unnamed x1, local copies, waits for them, and re-layouts: 1.57 us -> 0.66 us
where the time goes in v3:
time: 31.7 us; the launch traced here: 31.5 us
  Pallas kernels  30.8 us (97%)
  local copies, waits for them, and re-layouts  0.66 us (2%)
    pallas_call x1, Pallas kernels, local(): pl.pallas_call(functools.partial(kernel, ctx_size, tp_size), out_shape=pl...  30.8 us
    unnamed x1, local copies, waits for them, and re-layouts  0.66 us

profile of v3, /device:TPU:0, one launch (start us, length us, event | category | flops | bytes accessed | tf_op | source)
XLA Modules:
  0.0 31.5 jit_solution(2098303485344067620)
XLA Ops:
  0.0 30.8 %shard_map.91 = bf16[128,512]{1,0:T(8,128)(2,1)S(1)} custom-call(bf16[128,512]{1,0:T(8,128)(2,1)} %q_ref.1, bf16[128,128]{1,0:T(8,128)(2,1)} %k_ref.1, bf16[128,128]{1,0:T(8,128)(2,1)} %v_ref.1, bf16[128,512]{1,0:T(8,128)(2,1)} %o_ref.1, bf16[128,512]{1,0:T(8,128)(2,1)} %g_ref.1, bf16[2048,512]{1,0:T(8,128)(2,1)} %wq_ref.1, bf16[2048,128]{1,0:T(8,128)(2,1)} %wk_ref.1, ...), custom_call_target="tpu_custom_call" | custom-call | tf_op jit(solution)/shard_map/pallas_call | solution.py:415
  30.8 0.7 %copy.11 = bf16[128,512]{1,0:T(8,128)(2,1)} copy(bf16[128,512]{1,0:T(8,128)(2,1)S(1)} %shard_map.91) | data formatting | bytes 262144

commit v4 on v3

--- a/solution.py
+++ b/solution.py
@@ -72,6 +72,8 @@
     own_part,
     far_out,
     far_in,
+    tp_pair_out,
+    tp_pair_in,
     tp_out,
     tp_in,
     local_sem,
@@ -82,6 +84,8 @@
     pair_recv,
     far_send,
     far_recv,
+    tp_pair_send,
+    tp_pair_recv,
     tp_send,
     tp_recv,
     g_kv,
@@ -118,6 +122,13 @@
     def tp_peer(step):
         return lax.rem(t + step, tp_size)
 
+    tp_rows = tp_size // PAIR
+    t_row = lax.div(t, PAIR)
+    t_core = lax.rem(t, PAIR)
+
+    def tp_row(step):
+        return lax.rem(t_row + step, tp_rows)
+
     own_features = feature_rows(t)
     order = sorted(range(1, tp_size), key=lambda step: abs(step - tp_size // 2))
 
@@ -336,21 +347,41 @@
         [grad_query[:, head * rows : (head + 1) * rows] for head in range(heads)], axis=0
     )
 
+    def tp_pair_copy(row):
+        return pltpu.make_async_remote_copy(
+            src_ref=tp_pair_out.at[row],
+            dst_ref=tp_pair_in.at[row],
+            send_sem=tp_pair_send.at[row],
+            recv_sem=tp_pair_recv.at[row],
+            device_id=(c, t_row * PAIR + 1 - t_core),
+            device_id_type=MESH,
+        )
+
     def tp_copy(step):
         return pltpu.make_async_remote_copy(
             src_ref=tp_out.at[step - 1],
             dst_ref=tp_in.at[step - 1],
             send_sem=tp_send.at[step - 1],
             recv_sem=tp_recv.at[step - 1],
-            device_id=(c, tp_peer(step)),
-            device_id_type=MESH,
-        )
-
-    for step in order:
-        tp_out[step - 1] = nn_dot(wq[feature_rows(tp_peer(step)), :], stacked).astype(jnp.bfloat16)
+            device_id=(c, tp_row(step) * PAIR + t_core),
+            device_id_type=MESH,
+        )
+
+    def query_part(owner):
+        return nn_dot(wq[feature_rows(owner), :], stacked)
+
+    for step in range(1, tp_rows + 1):
+        row = tp_row(step)
+        tp_pair_out[row] = query_part(row * PAIR + 1 - t_core).astype(jnp.bfloat16)
+        tp_pair_copy(row).start()
+    for step in range(1, tp_rows):
+        row = tp_row(step)
+        part = query_part(row * PAIR + t_core)
+        tp_pair_copy(row).wait_recv()
+        tp_out[step - 1] = (part + tp_pair_in[row].astype(jnp.float32)).astype(jnp.bfloat16)
         tp_copy(step).start()
     each(far_size - 1, lambda i: send_far(0, i))
-    own_proj = nn_dot(wq[own_features, :], stacked)
+    own_proj = query_part(t)
 
     def grad_copy(step, kind):
         return pltpu.make_async_remote_copy(
@@ -375,7 +406,9 @@
             grad_copy(step, kind).start()
 
     finish(1)
-    for step in reversed(order):
+    tp_pair_copy(t_row).wait_recv()
+    own_proj += tp_pair_in[t_row].astype(jnp.float32)
+    for step in range(1, tp_rows):
         tp_copy(step).wait_recv()
         own_proj += tp_in[step - 1].astype(jnp.float32)
     total = own_proj.T
@@ -398,7 +431,9 @@
         for step in order:
             weight_copy(step, kind).wait_send()
             grad_copy(step, kind).wait_send()
-    for step in order:
+    for row in range(tp_rows):
+        tp_pair_copy(row).wait_send()
+    for step in range(1, tp_rows):
         tp_copy(step).wait_send()
 
 
@@ -437,8 +472,10 @@
             pltpu.VMEM((2, far_size) + block, full),
             pltpu.VMEM((2, far_size - 1) + block, low),
             pltpu.VMEM((2, far_size - 1) + block, low),
-            pltpu.VMEM((tp_size - 1, features, rows), low),
-            pltpu.VMEM((tp_size - 1, features, rows), low),
+            pltpu.VMEM((tp_size // PAIR, features, rows), low),
+            pltpu.VMEM((tp_size // PAIR, features, rows), low),
+            pltpu.VMEM((tp_size // PAIR - 1, features, rows), low),
+            pltpu.VMEM((tp_size // PAIR - 1, features, rows), low),
             dma((8,)),
             dma((2, far_size - 1)),
             dma((2, far_size)),
@@ -447,8 +484,10 @@
             dma((2, far_size)),
             dma((2, far_size - 1)),
             dma((2, far_size - 1)),
-            dma((tp_size - 1,)),
-            dma((tp_size - 1,)),
+            dma((tp_size // PAIR,)),
+            dma((tp_size // PAIR,)),
+            dma((tp_size // PAIR - 1,)),
+            dma((tp_size // PAIR - 1,)),
             pltpu.VMEM((tp_size, 2) + block, low),
             dma((tp_size - 1, 2)),
             dma((tp_size - 1, 2)),

time: 31.7 us -> 32.4 us (1.022)
  Pallas kernels: 30.8 us -> 31.4 us
    pallas_call x1, Pallas kernels: 30.8 us -> 31.4 us  [local(): pl.pallas_call(functools.partial(kernel, ctx_size, tp_size), out_shape=pl...]
where the time goes in v4:
time: 32.4 us; the launch traced here: 32 us
  Pallas kernels  31.4 us (97%)
  local copies, waits for them, and re-layouts  0.66 us (2%)
    pallas_call x1, Pallas kernels, local(): pl.pallas_call(functools.partial(kernel, ctx_size, tp_size), out_shape=pl...  31.4 us
    unnamed x1, local copies, waits for them, and re-layouts  0.66 us

profile of v4, /device:TPU:0, one launch (start us, length us, event | category | flops | bytes accessed | tf_op | source)
XLA Modules:
  0.0 32.0 jit_solution(4253444192144514273)
XLA Ops:
  0.0 31.4 %shard_map.91 = bf16[128,512]{1,0:T(8,128)(2,1)S(1)} custom-call(bf16[128,512]{1,0:T(8,128)(2,1)} %q_ref.1, bf16[128,128]{1,0:T(8,128)(2,1)} %k_ref.1, bf16[128,128]{1,0:T(8,128)(2,1)} %v_ref.1, bf16[128,512]{1,0:T(8,128)(2,1)} %o_ref.1, bf16[128,512]{1,0:T(8,128)(2,1)} %g_ref.1, bf16[2048,512]{1,0:T(8,128)(2,1)} %wq_ref.1, bf16[2048,128]{1,0:T(8,128)(2,1)} %wk_ref.1, ...), custom_call_target="tpu_custom_call" | custom-call | tf_op jit(solution)/shard_map/pallas_call | solution.py:450
  31.4 0.7 %copy.11 = bf16[128,512]{1,0:T(8,128)(2,1)} copy(bf16[128,512]{1,0:T(8,128)(2,1)S(1)} %shard_map.91) | data formatting | bytes 262144

commit v5 on v3

--- a/solution.py
+++ b/solution.py
@@ -12,12 +12,6 @@
 SCORE_SCALE = HEAD_SIZE ** (-0.5)
 LOG2_E = 1.4426950408889634
 MESH = pl.DeviceIdType.MESH
-
-
-def nt_dot(left, right):
-    return lax.dot_general(
-        left, right, (((1,), (1,)), ((), ())), preferred_element_type=jnp.float32
-    )
 
 
 def nn_dot(left, right):
@@ -61,6 +55,8 @@
     kv,
     q_rows,
     g_rows,
+    q_cols,
+    g_cols,
     delta,
     scores,
     grad_scores,
@@ -204,8 +200,10 @@
         lanes = slice(head * HEAD_SIZE, (head + 1) * HEAD_SIZE)
         held = slice(head * rows, (head + 1) * rows)
         q_rows[held, :] = q_in[:, lanes]
+        q_cols[:, held] = q_in[:, lanes].T
         g_head = g_in[:, lanes]
         g_rows[held, :] = g_head
+        g_cols[:, held] = g_head.T
         products = g_head.astype(jnp.float32) * o_in[:, lanes].astype(jnp.float32)
         delta[:, held] = jnp.sum(products.T, axis=0, keepdims=True)
 
@@ -220,7 +218,7 @@
     dq_t[...] = jnp.zeros_like(dq_t)
 
     def score_block(which, group, other):
-        raw = nt_dot(kv[0, group, other], q_rows[...]) * (SCORE_SCALE * LOG2_E)
+        raw = nn_dot(kv[0, group, other], q_cols[...]) * (SCORE_SCALE * LOG2_E)
         best = row_max[which]
         for part in range(2):
             key_pos = pos_ref[2 * (other * PAIR + group) + part] * span + key_offset
@@ -242,7 +240,7 @@
         target[1, other] = part.astype(target.dtype)
 
     def key_block(which, group, other):
-        grad_probs = nt_dot(kv[1, group, other], g_rows[...])
+        grad_probs = nn_dot(kv[1, group, other], g_cols[...])
         grads = (scores[which, other] * (grad_probs - delta[...])).astype(jnp.bfloat16)
         grad_scores[which, other] = grads
         part = nn_dot(grads, q_rows[...]) * SCORE_SCALE
@@ -370,7 +368,7 @@
         pair_copy(kind, a).wait_recv()
         own_part[kind, a] += pair_in[kind, a].astype(jnp.float32)
         each(far_size - 1, lambda i: add_far(kind, i))
-        g_kv[t, kind] = own_part[kind, a].astype(jnp.bfloat16)
+        g_kv[t, kind] = own_part[kind, a].T.astype(jnp.bfloat16)
         for step in order:
             grad_copy(step, kind).start()
 
@@ -378,28 +376,30 @@
     for step in reversed(order):
         tp_copy(step).wait_recv()
         own_proj += tp_in[step - 1].astype(jnp.float32)
-    total = own_proj.T
-    finish(0)
-    for kind in (1, 0):
-        local_copies[6 + kind].wait()
-        total += nt_dot(g_kv[t, kind], w_kv[t, kind])
-        for step in reversed(order):
-            sender = lax.rem(t + tp_size - step, tp_size)
-            weight_copy(step, kind).wait_recv()
-            grad_copy(step, kind).wait_recv()
-            total += nt_dot(g_kv[sender, kind], w_kv[sender, kind])
-    out_ref[...] = total.astype(out_ref.dtype)
-
     for kind in range(2):
         each(far_size - 1, lambda i, kind=kind: direct_copy(kind, i).wait_send())
         each(far_size, lambda i, kind=kind: forward(kind, b, i).wait_send())
         each(far_size, lambda i, kind=kind: pair_copy(kind, i).wait_send())
+        local_copies[6 + kind].wait()
+        for step in order:
+            weight_copy(step, kind).wait_recv()
+            weight_copy(step, kind).wait_send()
+    for step in order:
+        tp_copy(step).wait_send()
+    finish(0)
+    total = own_proj
+    for kind in (1, 0):
+        total += nn_dot(w_kv[t, kind], g_kv[t, kind])
+        for step in reversed(order):
+            sender = lax.rem(t + tp_size - step, tp_size)
+            grad_copy(step, kind).wait_recv()
+            total += nn_dot(w_kv[sender, kind], g_kv[sender, kind])
+    out_ref[...] = total.T.astype(out_ref.dtype)
+
+    for kind in range(2):
         each(far_size - 1, lambda i, kind=kind: far_copy(kind, i).wait_send())
         for step in order:
-            weight_copy(step, kind).wait_send()
             grad_copy(step, kind).wait_send()
-    for step in order:
-        tp_copy(step).wait_send()
 
 
 def local(ctx_size, tp_size, queries, key_rows, value_matrix, attention_out, output_grad, w_query, key_weight, value_weight, span_pos):
@@ -426,6 +426,8 @@
             pltpu.VMEM((2, PAIR, far_size) + block, low),
             pltpu.VMEM((query_rows, HEAD_SIZE), low),
             pltpu.VMEM((query_rows, HEAD_SIZE), low),
+            pltpu.VMEM((HEAD_SIZE, query_rows), low),
+            pltpu.VMEM((HEAD_SIZE, query_rows), low),
             pltpu.VMEM((1, query_rows), full),
             pltpu.VMEM((PAIR, far_size, rows, query_rows), full),
             pltpu.VMEM((PAIR, far_size, rows, query_rows), low),
@@ -449,7 +451,7 @@
             dma((2, far_size - 1)),
             dma((tp_size - 1,)),
             dma((tp_size - 1,)),
-            pltpu.VMEM((tp_size, 2) + block, low),
+            pltpu.VMEM((tp_size, 2, HEAD_SIZE, rows), low),
             dma((tp_size - 1, 2)),
             dma((tp_size - 1, 2)),
             dma((tp_size - 1, 2)),

time: 31.7 us -> 31.9 us (level)
  no operation moved by 1% of the time
where the time goes in v5:
time: 31.9 us; the launch traced here: 31.6 us
  Pallas kernels  30.9 us (97%)
  local copies, waits for them, and re-layouts  0.66 us (2%)
    pallas_call x1, Pallas kernels, local(): pl.pallas_call(functools.partial(kernel, ctx_size, tp_size), out_shape=pl...  30.9 us
    unnamed x1, local copies, waits for them, and re-layouts  0.66 us

profile of v5, /device:TPU:0, one launch (start us, length us, event | category | flops | bytes accessed | tf_op | source)
XLA Modules:
  0.0 31.6 jit_solution(17742520867148967865)
XLA Ops:
  0.0 30.9 %shard_map.91 = bf16[128,512]{1,0:T(8,128)(2,1)S(1)} custom-call(bf16[128,512]{1,0:T(8,128)(2,1)} %q_ref.1, bf16[128,128]{1,0:T(8,128)(2,1)} %k_ref.1, bf16[128,128]{1,0:T(8,128)(2,1)} %v_ref.1, bf16[128,512]{1,0:T(8,128)(2,1)} %o_ref.1, bf16[128,512]{1,0:T(8,128)(2,1)} %g_ref.1, bf16[2048,512]{1,0:T(8,128)(2,1)} %wq_ref.1, bf16[2048,128]{1,0:T(8,128)(2,1)} %wk_ref.1, ...), custom_call_target="tpu_custom_call" | custom-call | tf_op jit(solution)/shard_map/pallas_call | solution.py:415
  30.9 0.7 %copy.11 = bf16[128,512]{1,0:T(8,128)(2,1)} copy(bf16[128,512]{1,0:T(8,128)(2,1)S(1)} %shard_map.91) | data formatting | bytes 262144

commit v6 on v5

--- a/solution.py
+++ b/solution.py
@@ -176,9 +176,11 @@
             device_id_type=MESH,
         )
 
-    for kind in range(2):
-        each(far_size - 1, lambda i, kind=kind: direct_copy(kind, i).start())
+    def send_own(kind):
         own_forward(kind).start()
+        each(far_size - 1, lambda i: direct_copy(kind, i).start())
+
+    send_own(0)
 
     def weight_copy(step, kind):
         return pltpu.make_async_remote_copy(
@@ -190,7 +192,7 @@
             device_id_type=MESH,
         )
 
-    for kind in (1, 0):
+    def send_weights(kind):
         for step in order:
             weight_copy(step, kind).start()
 
@@ -271,9 +273,12 @@
     local_copies[3].wait()
     score_block(0, b, a)
     each(far_size - 1, key_arrival)
-    each(far_size - 1, value_arrival)
+    send_own(1)
+    send_weights(1)
     each(far_size, lambda i: exp_block(0, i))
     each(far_size, pair_key_arrival)
+    each(far_size - 1, value_arrival)
+    send_weights(0)
     row_max[1] = jnp.maximum(row_max[0], row_max[1])
     each(far_size, lambda i: exp_block(1, i))
     own_shrink = jnp.exp2(row_max[0] - row_max[1])

time: 31.9 us -> 34 us (1.066)
  Pallas kernels: 30.9 us -> 33.2 us
    pallas_call x1, Pallas kernels: 30.9 us -> 33.2 us  [local(): pl.pallas_call(functools.partial(kernel, ctx_size, tp_size), out_shape=pl...]
where the time goes in v6:
time: 34 us; the launch traced here: 33.9 us
  Pallas kernels  33.2 us (98%)
  local copies, waits for them, and re-layouts  0.66 us (2%)
    pallas_call x1, Pallas kernels, local(): pl.pallas_call(functools.partial(kernel, ctx_size, tp_size), out_shape=pl...  33.2 us

profile of v6, /device:TPU:0, one launch (start us, length us, event | category | flops | bytes accessed | tf_op | source)
XLA Modules:
  0.0 33.9 jit_solution(13211178847883445658)
XLA Ops:
  0.0 33.2 %shard_map.91 = bf16[128,512]{1,0:T(8,128)(2,1)S(1)} custom-call(bf16[128,512]{1,0:T(8,128)(2,1)} %q_ref.1, bf16[128,128]{1,0:T(8,128)(2,1)} %k_ref.1, bf16[128,128]{1,0:T(8,128)(2,1)} %v_ref.1, bf16[128,512]{1,0:T(8,128)(2,1)} %o_ref.1, bf16[128,512]{1,0:T(8,128)(2,1)} %g_ref.1, bf16[2048,512]{1,0:T(8,128)(2,1)} %wq_ref.1, bf16[2048,128]{1,0:T(8,128)(2,1)} %wk_ref.1, ...), custom_call_target="tpu_custom_call" | custom-call | tf_op jit(solution)/shard_map/pallas_call | solution.py:420
  33.2 0.7 %copy.11 = bf16[128,512]{1,0:T(8,128)(2,1)} copy(bf16[128,512]{1,0:T(8,128)(2,1)S(1)} %shard_map.91) | data formatting | bytes 262144

commit v7 on v5

--- a/solution.py
+++ b/solution.py
@@ -85,6 +85,7 @@
     w_recv,
     g_send,
     g_recv,
+    across_send,
 ):
     rows = q_ref.shape[0]
     span = rows // 2
@@ -103,7 +104,11 @@
     partner = (a * PAIR + 1 - b, t)
 
     def far(step):
-        return lax.rem(a + step, far_size)
+        other, bit = a, 1
+        while bit < far_size:
+            other = other + (step // bit % 2) * bit * (1 - 2 * (a // bit % 2))
+            bit *= 2
+        return other
 
     def far_device(other):
         return (other * PAIR + b, t)
@@ -252,28 +257,48 @@
         keys = kv[0, group, at].reshape(chunk_rows, HEAD_SIZE)
         dq_t[...] += tn_dot(keys, grad_scores[which, at].reshape(chunk_rows, query_rows))
 
+    def across(kind):
+        return pltpu.make_async_remote_copy(
+            src_ref=kv.at[kind, 1 - b, a],
+            dst_ref=kv.at[kind, 1 - b, a],
+            send_sem=across_send.at[kind],
+            recv_sem=kv_recv.at[kind, 1 - b, a],
+            device_id=far_device(far(1)),
+            device_id_type=MESH,
+        )
+
+    def pass_across(kind):
+        forward(kind, 1 - b, a).wait_recv()
+        across(kind).start()
+
     def key_arrival(i):
-        other = far(i + 1)
+        other = far(i + 2)
         forward(0, b, other).wait_recv()
         forward(0, b, other).start()
         score_block(0, b, other)
 
     def value_arrival(i):
-        other = far(i + 1)
+        other = far(i + 2)
         forward(1, b, other).wait_recv()
         forward(1, b, other).start()
 
     def pair_key_arrival(i):
-        other = far(i)
+        other = far(i + 1)
         forward(0, 1 - b, other).wait_recv()
         score_block(1, 1 - b, other)
 
     local_copies[3].wait()
     score_block(0, b, a)
-    each(far_size - 1, key_arrival)
-    each(far_size - 1, value_arrival)
+    pass_across(0)
+    each(far_size - 2, key_arrival)
+    forward(0, b, far(1)).wait_recv()
+    score_block(0, b, far(1))
+    pass_across(1)
+    each(far_size - 2, value_arrival)
+    forward(1, b, far(1)).wait_recv()
     each(far_size, lambda i: exp_block(0, i))
-    each(far_size, pair_key_arrival)
+    score_block(1, 1 - b, a)
+    each(far_size - 1, pair_key_arrival)
     row_max[1] = jnp.maximum(row_max[0], row_max[1])
     each(far_size, lambda i: exp_block(1, i))
     own_shrink = jnp.exp2(row_max[0] - row_max[1])
@@ -310,7 +335,7 @@
         far_copy(kind, i).start()
 
     def pair_value(i):
-        other = far(i + 1)
+        other = far(lax.rem(i + 1, far_size) if far_size > 8 else (i + 1) % far_size)
         value_block(1, other, pair_factor)
         pair_copy(1, other).start()
 
@@ -322,7 +347,9 @@
 
     each(far_size, pair_value)
     each(far_size, lambda i: value_block(0, i, own_factor))
-    each(far_size, pair_key)
+    each(far_size - 1, pair_key)
+    key_block(1, 1 - b, a)
+    pair_copy(0, a).start()
     each(far_size, lambda i: key_block(0, b, i))
     each(far_size - 1, lambda i: send_far(1, i))
 
@@ -378,7 +405,9 @@
         own_proj += tp_in[step - 1].astype(jnp.float32)
     for kind in range(2):
         each(far_size - 1, lambda i, kind=kind: direct_copy(kind, i).wait_send())
-        each(far_size, lambda i, kind=kind: forward(kind, b, i).wait_send())
+        own_forward(kind).wait_send()
+        across(kind).wait_send()
+        each(far_size - 2, lambda i, kind=kind: forward(kind, b, far(i + 2)).wait_send())
         each(far_size, lambda i, kind=kind: pair_copy(kind, i).wait_send())
         local_copies[6 + kind].wait()
         for step in order:
@@ -456,6 +485,7 @@
             dma((tp_size - 1, 2)),
             dma((tp_size - 1, 2)),
             dma((tp_size - 1, 2)),
+            dma((2,)),
         ],
         compiler_params=pltpu.CompilerParams(
             collective_id=0, has_side_effects=True, vmem_limit_bytes=(65536 - 192) * 1024

time: 31.9 us -> 32.4 us (1.016)
  Pallas kernels: 30.9 us -> 31.6 us
    pallas_call x1, Pallas kernels: 30.9 us -> 31.6 us  [local(): pl.pallas_call(functools.partial(kernel, ctx_size, tp_size), out_shape=pl...]
where the time goes in v7:
time: 32.4 us; the launch traced here: 32.3 us
  Pallas kernels  31.6 us (98%)
  local copies, waits for them, and re-layouts  0.66 us (2%)
    pallas_call x1, Pallas kernels, local(): pl.pallas_call(functools.partial(kernel, ctx_size, tp_size), out_shape=pl...  31.6 us
    unnamed x1, local copies, waits for them, and re-layouts  0.66 us

profile of v7, /device:TPU:0, one launch (start us, length us, event | category | flops | bytes accessed | tf_op | source)
XLA Modules:
  0.0 32.3 jit_solution(923470577478202147)
XLA Ops:
  0.0 31.6 %shard_map.91 = bf16[128,512]{1,0:T(8,128)(2,1)S(1)} custom-call(bf16[128,512]{1,0:T(8,128)(2,1)} %q_ref.1, bf16[128,128]{1,0:T(8,128)(2,1)} %k_ref.1, bf16[128,128]{1,0:T(8,128)(2,1)} %v_ref.1, bf16[128,512]{1,0:T(8,128)(2,1)} %o_ref.1, bf16[128,512]{1,0:T(8,128)(2,1)} %g_ref.1, bf16[2048,512]{1,0:T(8,128)(2,1)} %wq_ref.1, bf16[2048,128]{1,0:T(8,128)(2,1)} %wk_ref.1, ...), custom_call_target="tpu_custom_call" | custom-call | tf_op jit(solution)/shard_map/pallas_call | solution.py:444
  31.6 0.7 %copy.11 = bf16[128,512]{1,0:T(8,128)(2,1)} copy(bf16[128,512]{1,0:T(8,128)(2,1)S(1)} %shard_map.91) | data formatting | bytes 262144

commit v8 on v3

--- a/solution.py
+++ b/solution.py
@@ -194,10 +194,6 @@
             device_id_type=MESH,
         )
 
-    for kind in (1, 0):
-        for step in order:
-            weight_copy(step, kind).start()
-
     for copy in local_copies[:3]:
         copy.wait()
     for head in range(heads):
@@ -274,6 +270,9 @@
     score_block(0, b, a)
     each(far_size - 1, key_arrival)
     each(far_size - 1, value_arrival)
+    for kind in (1, 0):
+        for step in order:
+            weight_copy(step, kind).start()
     each(far_size, lambda i: exp_block(0, i))
     each(far_size, pair_key_arrival)
     row_max[1] = jnp.maximum(row_max[0], row_max[1])

time: 31.7 us -> 35.4 us (1.12)
  Pallas kernels: 30.8 us -> 34.6 us
    pallas_call x1, Pallas kernels: 30.8 us -> 34.6 us  [local(): pl.pallas_call(functools.partial(kernel, ctx_size, tp_size), out_shape=pl...]
where the time goes in v8:
time: 35.4 us; the launch traced here: 35.3 us
  Pallas kernels  34.6 us (98%)
  local copies, waits for them, and re-layouts  0.66 us (2%)
    pallas_call x1, Pallas kernels, local(): pl.pallas_call(functools.partial(kernel, ctx_size, tp_size), out_shape=pl...  34.6 us

profile of v8, /device:TPU:0, one launch (start us, length us, event | category | flops | bytes accessed | tf_op | source)
XLA Modules:
  0.0 35.3 jit_solution(3650161521791909605)
XLA Ops:
  0.0 34.6 %shard_map.91 = bf16[128,512]{1,0:T(8,128)(2,1)S(1)} custom-call(bf16[128,512]{1,0:T(8,128)(2,1)} %q_ref.1, bf16[128,128]{1,0:T(8,128)(2,1)} %k_ref.1, bf16[128,128]{1,0:T(8,128)(2,1)} %v_ref.1, bf16[128,512]{1,0:T(8,128)(2,1)} %o_ref.1, bf16[128,512]{1,0:T(8,128)(2,1)} %g_ref.1, bf16[2048,512]{1,0:T(8,128)(2,1)} %wq_ref.1, bf16[2048,128]{1,0:T(8,128)(2,1)} %wk_ref.1, ...), custom_call_target="tpu_custom_call" | custom-call | tf_op jit(solution)/shard_map/pallas_call | solution.py:414
  34.6 0.7 %copy.11 = bf16[128,512]{1,0:T(8,128)(2,1)} copy(bf16[128,512]{1,0:T(8,128)(2,1)S(1)} %shard_map.91) | data formatting | bytes 262144
